TPU v7x, 768 devices: a whole 4x8x12 slice. The times are simulated.
768 devices in a mesh: pair: 48 (over z, x_hi, core), blk: 8 (over y), rep: 2 (over x_lo).
Axes of the slice: x: 4 (x_hi: 2, x_lo: 2; x = x_hi * 2 + x_lo), y: 8, z: 12, core: 2. Of those that a mesh axis runs over, the one named last changes fastest.
Arguments:
- amplitudes: bfloat16 [6144, 6144], P('pair'), may hold values from -6 to 6
- tile_map: int32 [48, 48], replicated, may hold values 0 or 1
- ladder_ints: bfloat16 [6144, 48, 128], P('rep', None, 'blk'), may hold values from -0.078125 to 0.078125
- hole_ints: bfloat16 [48, 128, 6144], P(None, ('blk', 'rep')), may hold values from -0.078125 to 0.078125
Outputs:
- residual: bfloat16 [48, 48, 128, 128], P('pair', None, ('blk', 'rep'))
Inputs may be any that keep to these rules, and one draw needn't show every extreme that they name: tile_map holds only 0 and 1.
All inputs are finite; a program needn't handle non-finite values.
Results may differ from a plain program's by a relative error of at most 0.001.
Values may be sent and summed in bfloat16 or wider, within the bound.
A program may use at most 32 MiB of HBM per device.

v0:
```python
import jax
import jax.numpy as jnp
from jax import lax
from jax.sharding import PartitionSpec as P


def tile_order(tile_map):
    counts = jnp.sum(tile_map, axis=0)
    tile_ids = jnp.arange(tile_map.shape[1], dtype=jnp.int32)
    scores = counts * tile_map.shape[1] + tile_ids
    return jnp.argsort(-scores, stable=True)


def per_device(amplitudes, tile_map, ladder_ints, hole_ints):
    row_count, width = amplitudes.shape
    tile_count = tile_map.shape[0]
    tile_width = width // tile_count
    pair_index = lax.axis_index("pair")
    kept_tiles = lax.dynamic_slice_in_dim(tile_map, pair_index, 1, 0)[0]
    blocks = amplitudes.reshape(row_count, tile_count, tile_width)
    masked = blocks * kept_tiles.astype(amplitudes.dtype)[None, :, None]
    chosen_blocks = tile_order(tile_map)
    ordered = jnp.take(masked, chosen_blocks, axis=1)
    half_rows = ladder_ints.shape[0]
    share_width = ladder_ints.shape[2]
    half_start = lax.axis_index("rep") * half_rows
    own_columns = lax.dynamic_slice_in_dim(
        masked.reshape(row_count, width), half_start, half_rows, 1
    )
    partial_value = jnp.dot(
        own_columns,
        ladder_ints.reshape(half_rows, tile_count * share_width),
        preferred_element_type=jnp.float32,
    )
    partial_ordered = jnp.take(
        partial_value.reshape(row_count, tile_count, share_width), chosen_blocks, axis=1
    )
    arrived = lax.all_to_all(partial_ordered, "pair", split_axis=1, concat_axis=0, tiled=True)
    blk_count = lax.axis_size("blk")
    rep_count = lax.axis_size("rep")
    local_rows = hole_ints.shape[1]
    split_rows = arrived.reshape(tile_count, blk_count, rep_count, local_rows, share_width)
    moved = lax.all_to_all(split_rows, "blk", split_axis=1, concat_axis=4, tiled=True)
    summed = lax.psum_scatter(moved, "rep", scatter_dimension=2, tiled=True)
    ladder_term = summed.reshape(tile_count, local_rows, tile_width)
    flat_hole = hole_ints.reshape(tile_count * local_rows, hole_ints.shape[2])
    column = lax.all_to_all(ordered, "pair", split_axis=1, concat_axis=0, tiled=True)
    product = jnp.dot(flat_hole, column[:, 0, :], preferred_element_type=jnp.float32)
    hole_term = product.reshape(tile_count, local_rows, column.shape[2])
    combined = (ladder_term + hole_term).astype(jnp.bfloat16)
    return combined[None]


def solution(mesh):
    placed = (P("pair", None), P(), P("rep", None, "blk"), P(None, ("blk", "rep"), None))
    return jax.shard_map(
        per_device,
        mesh=mesh,
        in_specs=placed,
        out_specs=P("pair", None, ("blk", "rep"), None),
        check_vma=False,
    )
```

profile of v0, /device:TPU:1, one launch (start us, length us, event | category | flops | bytes accessed | tf_op | source)
XLA Modules:
  0.0 158.7 jit_solution(10911236143639003960)
XLA Ops:
  6.5 0.8 reduce_sum.9
  7.3 2.0 %sort.17 = (s32[48]{0:T(128)}, s32[48]{0:T(128)S(1)}) sort(s32[48]{0:T(128)S(1)} %add_negate_fusion, s32[48]{0:T(128)S(1)} %iota.8), dimensions={0}, to_apply=%region_1.0 | sort | flops 288 | bytes 768 | tf_op jit(solution)/shard_map/jit(argsort)/sort | solution.py:11
  9.4 0.7 convert_bitcast_fusion
  10.1 0.1 broadcast_bitcast_fusion
  10.2 4.0 %fusion = f32[128,48,16]{0,2,1:T(8,128)S(1)} fusion(bf16[3072,48,16]{0,2,1:T(8,128)(2,1)} %param.6, bf16[128,6144]{1,0:T(8,128)(2,1)} %param.4, s32[]{:T(128)S(6)} %select_n.23, bf16[3072]{0:T(1024)(128)(2,1)S(1)} %dynamic-slice), kind=kOutput, calls=%fused_computation.2 | convolution fusion | flops 605552640 | bytes 5904388 | tf_op jit(solution)/shard_map/dot_general | solution.py:30
  14.1 0.6 gather_fusion
  14.7 0.1 select_bitcast_fusion.1
  14.9 42.0 %all_to_all.48 = f32[128,48,16]{0,2,1:T(8,128)S(1)} all-to-all(f32[128,48,16]{0,2,1:T(8,128)S(1)} %select_bitcast_fusion.1), channel_id=1, replica_groups=mesh['pair'=48,'blk'=8,'rep'=2] {'pair'}, dimensions={1} | all-to-all | bytes 786432 | tf_op jit(solution)/shard_map/all_to_all | solution.py:38
  56.9 0.0 copy-start
  56.9 0.6 copy.25
  57.4 1.7 %reshape.80 = f32[8,1,12288]{2,1,0:T(1,128)} reshape(f32[8,2,8,16,48]{4,3,2,1,0:T(8,128)S(1)} %bitcast.52) | data formatting | bytes 786432
  59.2 6.8 %all-to-all-start.1 = ((f32[8,1,12288]{2,1,0:T(1,128)}), f32[8,1,12288]{2,1,0:T(1,128)S(1)}, u32[]{:S(2)}, u32[]{:S(2)}) async-start(f32[8,1,12288]{2,1,0:T(1,128)} %reshape.80), calls=%async_computation.1 | async-start | bytes 786432 | tf_op jit(solution)/shard_map/all_to_all | solution.py:43
  66.0 0.0 copy-done
  66.0 0.9 copy.28
  66.9 0.9 copy.29
  67.8 0.2 broadcast_multiply_fusion
  68.0 0.8 gather_fusion.1
  68.8 1.4 select_bitcast_fusion
  70.2 10.9 %all-to-all-done.1 = f32[8,1,12288]{2,1,0:T(1,128)S(1)} async-done(((f32[8,1,12288]{2,1,0:T(1,128)}), f32[8,1,12288]{2,1,0:T(1,128)S(1)}, u32[]{:S(2)}, u32[]{:S(2)}) %all-to-all-start.1) | async-done | bytes 393248 | tf_op jit(solution)/shard_map/all_to_all | solution.py:43
  81.1 4.6 %all-to-all-start.2 = ((bf16[128,48,128]{2,0,1:T(8,128)(2,1)}), bf16[128,48,128]{2,0,1:T(8,128)(2,1)S(1)}, u32[]{:S(2)}, u32[]{:S(2)}) async-start(bf16[128,48,128]{2,0,1:T(8,128)(2,1)} %select_bitcast_fusion), calls=%async_computation.3 | async-start | bytes 3145728 | tf_op jit(solution)/shard_map/all_to_all | solution.py:47
  85.8 0.0 reduce-scatter.2.cloned.1.call-start
  85.8 0.5 broadcast.21
  86.3 1.6 reduce
  87.9 0.5 reshape.81
  88.4 0.1 bitcast_bitcast_fusion
  88.5 0.1 copy.26
  88.6 1.1 copy.27
  89.6 0.0 reduce-scatter.2.cloned.1.call-update
  89.7 56.6 %all-to-all-done.2 = bf16[128,48,128]{2,0,1:T(8,128)(2,1)S(1)} async-done(((bf16[128,48,128]{2,0,1:T(8,128)(2,1)}), bf16[128,48,128]{2,0,1:T(8,128)(2,1)S(1)}, u32[]{:S(2)}, u32[]{:S(2)}) %all-to-all-start.2) | async-done | bytes 1572896 | tf_op jit(solution)/shard_map/all_to_all | solution.py:47
  146.3 3.9 %fusion.4 = f32[384,128]{0,1:T(8,128)S(1)} fusion(bf16[6144,128]{1,0:T(8,128)(2,1)S(1)} %bitcast.51, bf16[48,8,6144]{2,1,0:T(8,128)(2,1)} %param.7), kind=kOutput, calls=%fused_computation.7 | convolution fusion | flops 603979776 | bytes 6488064 | tf_op jit(solution)/shard_map/dot_general | solution.py:48
  150.1 0.1 copy.30
  150.3 0.0 reduce-scatter.2.cloned.1.call-done
  150.3 1.6 %fusion.10 = bf16[1,48,8,128]{3,2,1,0:T(8,128)(2,1)} fusion(f32[384,128]{1,0:T(8,128)S(1)} %copy.30, f32[48,1,1,8,128]{4,3,0,2,1:T(8,128)} %reduce-scatter.2.cloned.1.call-done), kind=kLoop, calls=%fused_computation.14 | loop fusion | flops 98304 | bytes 491520 | tf_op jit(solution)/shard_map/convert_element_type | solution.py:50
  (6 shorter events, 0.0 us)
Async XLA Ops:
  56.9 9.1 %copy-start = (bf16[128,6144]{1,0:T(8,128)(2,1)S(1)}, bf16[128,6144]{1,0:T(8,128)(2,1)}, u32[]{:S(2)}) copy-start(bf16[128,6144]{1,0:T(8,128)(2,1)} %param.4) | copy-start | bytes 4718596
  59.2 22.0 %all-to-all-start.1 = ((f32[8,1,12288]{2,1,0:T(1,128)}), f32[8,1,12288]{2,1,0:T(1,128)S(1)}, u32[]{:S(2)}, u32[]{:S(2)}) async-start(f32[8,1,12288]{2,1,0:T(1,128)} %reshape.80), calls=%async_computation.1 | async-start | bytes 786432 | tf_op jit(solution)/shard_map/all_to_all | solution.py:43
  81.1 65.1 %all-to-all-start.2 = ((bf16[128,48,128]{2,0,1:T(8,128)(2,1)}), bf16[128,48,128]{2,0,1:T(8,128)(2,1)S(1)}, u32[]{:S(2)}, u32[]{:S(2)}) async-start(bf16[128,48,128]{2,0,1:T(8,128)(2,1)} %select_bitcast_fusion), calls=%async_computation.3 | async-start | bytes 3145728 | tf_op jit(solution)/shard_map/all_to_all | solution.py:47
  85.8 64.5 %reduce-scatter.2.cloned.1.call-start = ((), (), s32[]{:S(2)}) async-start(), calls=%async_computation.4 | async-start | bytes 589824 | tf_op jit(solution)/shard_map/reduce_scatter | solution.py:44
Sparse Core Ops, SparseCore 0:
  89.8 20.8 reduce-scatter.1
where the time goes:
time: 159 us
  waiting for transfers between devices  67.6 us (43%)
  blocking collectives  42 us (26%)
  between operations  13.6 us (9%)
  starting transfers between devices  11.5 us (7%)
  other arithmetic  8.33 us (5%)
  local copies, waits for them, and re-layouts  7.98 us (5%)
  matrix products  7.82 us (5%)
    all_to_all x1, waiting for transfers between devices, per_device(): lax.all_to_all(ordered, 'pair', split_axis=1, concat_axis=0, tiled=True)  56.6 us
    all_to_all x1, blocking collectives, per_device(): lax.all_to_all(partial_ordered, 'pair', split_axis=1, concat_axis=0, tile...  42 us
    all_to_all x1, waiting for transfers between devices, per_device(): lax.all_to_all(split_rows, 'blk', split_axis=1, concat_axis=4, tiled=True)  10.9 us
    all_to_all x1, starting transfers between devices, per_device(): lax.all_to_all(split_rows, 'blk', split_axis=1, concat_axis=4, tiled=True)  6.82 us
    all_to_all x1, starting transfers between devices, per_device(): lax.all_to_all(ordered, 'pair', split_axis=1, concat_axis=0, tiled=True)  4.62 us
    dot_general x1, matrix products, per_device(): jnp.dot(own_columns, ladder_ints.reshape(half_rows, tile_count * share_wi...  3.97 us
    dot_general x1, matrix products, per_device(): jnp.dot(flat_hole, column[:, 0, :], preferred_element_type=jnp.float32)  3.85 us
  transfers between devices with their start and end apart: 3, of which 2 were waited for; matrix products, arithmetic and copies ran while one was open for 8% of the time, Pallas kernels for 0%

commit v1 on v0

v1 whole, which is shorter than its diff:
```python
import functools

import jax
import jax.numpy as jnp
from jax import lax
from jax.experimental import pallas as pl
from jax.experimental.pallas import tpu as pltpu
from jax.sharding import PartitionSpec as P

MESH = pl.DeviceIdType.MESH
F32 = jnp.float32
BF16 = jnp.bfloat16


def tile_order_and_mask(tm_ref, pair_index, tiles):
    tm = tm_ref[...]
    lane = lax.broadcasted_iota(jnp.int32, (tiles, tiles), 1)
    sub = lax.broadcasted_iota(jnp.int32, (tiles, tiles), 0)
    score_row = jnp.sum(tm, axis=0, keepdims=True) * tiles + lane[:1]
    spread = jnp.broadcast_to(score_row, (tiles, tiles))
    score_col = jnp.sum(jnp.where(lane == sub, spread, 0), axis=1, keepdims=True)
    rank_col = jnp.sum((spread > score_col).astype(jnp.int32), axis=1, keepdims=True)
    order_row = jnp.sum(jnp.where(rank_col == lane, sub, 0), axis=0, keepdims=True)
    mask_row = tm_ref[pl.ds(pair_index, 1), :]
    mask_col = jnp.sum(
        jnp.where(lane == sub, jnp.broadcast_to(mask_row, (tiles, tiles)), 0), axis=1, keepdims=True)
    kept_row = jnp.sum(jnp.where(rank_col == lane, mask_col, 0), axis=0, keepdims=True)
    return order_row, mask_row, kept_row


def swap_lane_blocks(rows, block):
    n = len(rows)
    width = n * block
    lane = lax.broadcasted_iota(jnp.int32, rows[0].shape, 1) // block
    d = n // 2
    while d:
        keep = (lane & d) == 0
        out = list(rows)
        for a in range(n):
            if a & d:
                continue
            b = a + d
            out[a] = jnp.where(keep, rows[a], pltpu.roll(rows[b], d * block, 1))
            out[b] = jnp.where(keep, pltpu.roll(rows[a], width - d * block, 1), rows[b])
        rows = out
        d //= 2
    return rows


def kernel(dims, a_hbm, tm_hbm, l_hbm, h_hbm, out_ref,
           a_ref, tm_ref, l_ref, h_ref, am_ref, meta_ref, meta_smem,
           hsend, panel, psend, prep, ysend, yrecv, vt, qsend, pfin,
           load_sem, meta_sem, h1_send, h1_recv, x_send, x_recv, ring_send, ring_recv,
           p2_send, p2_recv, p3_send, p3_recv, p4_send, p4_recv):
    tiles, n_blk, share, width = dims
    half_tiles = tiles // 2
    p = lax.axis_index("pair")
    y = lax.axis_index("blk")
    x = lax.axis_index("rep")
    core = lax.rem(p, 2)
    zz = p // 2
    other_x = 1 - x
    up = lax.rem(y + 1, n_blk)
    down = lax.rem(y + n_blk - 1, n_blk)

    loads = [
        pltpu.make_async_copy(tm_hbm, tm_ref, load_sem.at[0]),
        pltpu.make_async_copy(l_hbm, l_ref, load_sem.at[1]),
        pltpu.make_async_copy(h_hbm, h_ref, load_sem.at[2]),
    ]
    loads[0].start()

    @pl.loop(0, tiles)
    def _(v):
        start = pl.multiple_of(v * width, width)
        pltpu.make_async_copy(a_hbm.at[:, pl.ds(start, width)], a_ref.at[v], load_sem.at[3]).start()

    loads[1].start()
    loads[2].start()

    barrier = pltpu.get_barrier_semaphore()

    @pl.loop(1, tiles)
    def _(j):
        q = lax.rem(p + j, tiles)
        pl.semaphore_signal(barrier, inc=1, device_id=(q, y, x), device_id_type=MESH)

    @pl.loop(1, n_blk)
    def _(j):
        pl.semaphore_signal(barrier, inc=1, device_id=(p, lax.rem(y + j, n_blk), x), device_id_type=MESH)

    pl.semaphore_signal(barrier, inc=1, device_id=(p, y, other_x), device_id_type=MESH)

    loads[0].wait()
    order_row, mask_row, kept_row = tile_order_and_mask(tm_ref, p, tiles)
    meta_ref[0:1, 0:tiles] = order_row
    meta_ref[1:2, 0:tiles] = mask_row
    meta_ref[2:3, 0:tiles] = kept_row
    to_smem = pltpu.make_async_copy(meta_ref, meta_smem, meta_sem)
    to_smem.start()
    to_smem.wait()
    pltpu.make_async_copy(a_ref, a_ref, load_sem.at[3]).wait()

    parity = lax.rem(core + x, 2)
    rows16 = pl.ds(pl.multiple_of(y * 16, 16), 16)
    for j in range(half_tiles):
        piece = a_ref[meta_smem[0, 2 * j + parity], rows16, :]
        kept = meta_smem[2, 2 * j + parity].astype(F32)
        hsend[j] = (piece.astype(F32) * kept).astype(BF16)

    pl.semaphore_wait(barrier, tiles - 1 + n_blk - 1 + 1)

    @pl.when(x == 0)
    def _():
        pltpu.make_async_copy(hsend.at[zz], panel.at[x, y, zz], h1_recv).start()

    @pl.when(x != 0)
    def _():
        pltpu.make_async_remote_copy(
            hsend.at[zz], panel.at[x, y, zz], h1_send, h1_recv,
            device_id=(2 * zz + parity, y, x), device_id_type=MESH).start()

    @pl.loop(1, half_tiles)
    def _(j):
        dest = lax.rem(zz + j, half_tiles)
        pltpu.make_async_remote_copy(
            hsend.at[dest], panel.at[x, y, zz], h1_send, h1_recv,
            device_id=(2 * dest + parity, y, x), device_id_type=MESH).start()

    for j in range(half_tiles):
        kept = meta_smem[1, x * half_tiles + j].astype(F32)
        am_ref[:, j * width:(j + 1) * width] = (
            a_ref[x * half_tiles + j].astype(F32) * kept).astype(BF16)
    loads[1].wait()
    cols = tiles * share
    step_cols = 256
    for n in range(cols // step_cols):
        part = lax.dot_general(
            am_ref[...], l_ref[n * step_cols:(n + 1) * step_cols, :],
            (((1,), (1,)), ((), ())), preferred_element_type=F32)
        part = part.reshape(n_blk, 2, 8, step_cols)
        for s in range(2):
            psend[s, :, :, n * step_cols:(n + 1) * step_cols] = part[:, s]
    p2 = pltpu.make_async_remote_copy(
        psend.at[other_x], prep, p2_send, p2_recv,
        device_id=(p, y, other_x), device_id_type=MESH)
    p2.start()

    def slot(origin_x, origin_y):
        return panel.at[origin_x, lax.rem(origin_y + 2 * n_blk, n_blk)]

    def ring(step, part, direction):
        origin = x if part == 0 else other_x
        at = y - (step - 1) if direction == 0 else y + (step - 1)
        which = ((step - 1) * 2 + part) * 2 + direction
        return pltpu.make_async_remote_copy(
            slot(origin, at), slot(origin, at), ring_send.at[which], ring_recv.at[which],
            device_id=(p, up if direction == 0 else down, x), device_id_type=MESH)

    copies = {}

    def go(step, part, direction):
        if step > 1:
            copies[(step - 1, part, direction)].wait_recv()
        copies[(step, part, direction)] = ring(step, part, direction)
        copies[(step, part, direction)].start()

    mine = panel.at[x, y]
    pltpu.make_async_copy(mine, mine, h1_recv).wait()
    swap = pltpu.make_async_remote_copy(
        mine, mine, x_send, x_recv, device_id=(p, y, other_x), device_id_type=MESH)
    swap.start()
    go(1, 0, 0)
    go(1, 0, 1)
    swap.wait_recv()
    go(1, 1, 0)
    go(1, 1, 1)

    p2.wait_recv()
    ysend[...] = psend[x] + prep[...]

    @pl.loop(1, n_blk)
    def _(j):
        dest = lax.rem(y + j, n_blk)
        pltpu.make_async_remote_copy(
            ysend.at[dest], yrecv.at[y], p3_send, p3_recv,
            device_id=(p, dest, x), device_id_type=MESH).start()

    pltpu.make_async_copy(ysend.at[y], yrecv.at[y], p3_recv).start()

    for part in range(2):
        for direction in range(2):
            go(2, part, direction)

    pltpu.make_async_copy(yrecv, yrecv, p3_recv).wait()
    per = width // share
    for g in range(cols // width):
        rows = [yrecv[b, :, g * width:(g + 1) * width] for b in range(n_blk)]
        for k, row in enumerate(swap_lane_blocks(rows, share)):
            vt[g * per + k] = row
    for q in range(tiles):
        qsend[q] = vt[meta_smem[0, q]]

    @pl.loop(1, tiles)
    def _(j):
        q = lax.rem(p + j, tiles)
        pltpu.make_async_remote_copy(
            qsend.at[q], pfin.at[p], p4_send, p4_recv,
            device_id=(q, y, x), device_id_type=MESH).start()

    pltpu.make_async_copy(qsend.at[p], pfin.at[p], p4_recv).start()

    for part in range(2):
        for direction in range(2):
            go(3, part, direction)
    go(4, 0, 0)
    go(4, 1, 1)
    copies[(3, 0, 1)].wait_recv()
    copies[(3, 1, 0)].wait_recv()
    copies[(4, 0, 0)].wait_recv()
    copies[(4, 1, 1)].wait_recv()
    loads[2].wait()
    rows_out = out_ref.shape[0]
    acc = jnp.zeros((rows_out, width), F32)
    for j in range(half_tiles):
        even = panel[core, :, j].reshape(width, width)
        odd = panel[1 - core, :, j].reshape(width, width)
        acc += jnp.dot(
            h_ref[:, 2 * j * width:2 * (j + 1) * width],
            jnp.concatenate([even, odd], axis=0), preferred_element_type=F32)

    pltpu.make_async_copy(pfin, pfin, p4_recv).wait()
    out_ref[...] = (acc + pfin[...].reshape(rows_out, width)).astype(BF16)

    @pl.when(x == 0)
    def _():
        sent = hsend.at[pl.ds(0, half_tiles - 1)]
        pltpu.make_async_copy(sent, sent, h1_send).wait()

    @pl.when(x != 0)
    def _():
        pltpu.make_async_copy(hsend, hsend, h1_send).wait()

    swap.wait_send()
    p2.wait_send()
    for copy in copies.values():
        copy.wait_send()
    sent = ysend.at[pl.ds(0, n_blk - 1)]
    pltpu.make_async_copy(sent, sent, p3_send).wait()
    sent = qsend.at[pl.ds(0, tiles - 1)]
    pltpu.make_async_copy(sent, sent, p4_send).wait()


def per_device(amplitudes, tile_map, ladder_ints, hole_ints):
    rows, total = amplitudes.shape
    tiles = tile_map.shape[0]
    width = total // tiles
    half_rows, _, share = ladder_ints.shape
    n_blk = width // share
    local_rows = hole_ints.shape[1]
    ladder = jnp.transpose(ladder_ints, (1, 2, 0)).reshape(tiles * share, half_rows)
    holes = hole_ints.reshape(tiles * local_rows, hole_ints.shape[2])
    dma = pltpu.SemaphoreType.DMA
    out = pl.pallas_call(
        functools.partial(kernel, (tiles, n_blk, share, width)),
        out_shape=jax.ShapeDtypeStruct((tiles * local_rows, width), BF16),
        in_specs=[pl.BlockSpec(memory_space=pl.ANY)] * 4,
        out_specs=pl.BlockSpec(memory_space=pltpu.VMEM),
        scratch_shapes=[
            pltpu.VMEM((tiles, rows, width), BF16),
            pltpu.VMEM((tiles, tiles), jnp.int32),
            pltpu.VMEM(ladder.shape, BF16),
            pltpu.VMEM(holes.shape, BF16),
            pltpu.VMEM((rows, half_rows), BF16),
            pltpu.VMEM((8, 128), jnp.int32),
            pltpu.SMEM((8, 128), jnp.int32),
            pltpu.VMEM((tiles // 2, 16, width), BF16),
            pltpu.VMEM((2, n_blk, tiles // 2, 16, width), BF16),
            pltpu.VMEM((2, n_blk, 8, tiles * share), F32),
            pltpu.VMEM((n_blk, 8, tiles * share), F32),
            pltpu.VMEM((n_blk, 8, tiles * share), F32),
            pltpu.VMEM((n_blk, 8, tiles * share), F32),
            pltpu.VMEM((tiles, 8, width), F32),
            pltpu.VMEM((tiles, 8, width), F32),
            pltpu.VMEM((tiles, 8, width), F32),
            dma((4,)), dma(()), dma(()), dma(()), dma(()), dma(()), dma((16,)), dma((16,)),
            dma(()), dma(()), dma(()), dma(()), dma(()), dma(()),
        ],
        compiler_params=pltpu.CompilerParams(
            collective_id=0, has_side_effects=True, vmem_limit_bytes=32 * 1024 * 1024),
        cost_estimate=pl.CostEstimate(flops=1_300_000_000, bytes_accessed=12_000_000, transcendentals=0),
    )(amplitudes, tile_map, ladder, holes)
    return out.reshape(1, tiles, local_rows, width)


def solution(mesh):
    placed = (P("pair", None), P(), P("rep", None, "blk"), P(None, ("blk", "rep"), None))
    return jax.shard_map(
        per_device,
        mesh=mesh,
        in_specs=placed,
        out_specs=P("pair", None, ("blk", "rep"), None),
        check_vma=False,
    )
```

time: 159 us -> 65.8 us (0.41)
  waiting for transfers between devices: 67.6 us -> 0 us
  Pallas kernels: 0 us -> 58.1 us
  blocking collectives: 42 us -> 0 us
  between operations: 13.6 us -> 0.01 us
  starting transfers between devices: 11.5 us -> 0 us
  other arithmetic: 8.33 us -> 0 us
  matrix products: 7.82 us -> 0 us
    all_to_all x2 -> x0, waiting for transfers between devices: 67.5 us -> none  [the longest x1 56.6 us: per_device(): lax.all_to_all(ordered, 'pair', split_axis=1, concat_axis=0, tiled=True)]
    pallas_call x0 -> x1, Pallas kernels: none -> 58.1 us  [per_device(): pl.pallas_call(functools.partial(kernel, (tiles, n_blk, share, width)), o...]
    all_to_all x1 -> x0, blocking collectives: 42 us -> none  [per_device(): lax.all_to_all(partial_ordered, 'pair', split_axis=1, concat_axis=0, tile...]
    all_to_all x2 -> x0, starting transfers between devices: 11.4 us -> none  [the longest x1 6.82 us: per_device(): lax.all_to_all(split_rows, 'blk', split_axis=1, concat_axis=4, tiled=True)]
    dot_general x2 -> x0, matrix products: 7.82 us -> none  [the longest x1 3.97 us: per_device(): jnp.dot(own_columns, ladder_ints.reshape(half_rows, tile_count * share_wi...]
    unnamed x5 -> x9, local copies, waits for them, and re-layouts: 3.09 us -> 7.46 us
    all_to_all x5 -> x0, local copies, waits for them, and re-layouts: 2.34 us -> none  [the longest x4 1.78 us: per_device(): lax.all_to_all(split_rows, 'blk', split_axis=1, concat_axis=4, tiled=True)]
    convert_element_type x2 -> x0, other arithmetic: 2.29 us -> none  [the longest x1 1.59 us: per_device(): combined = (ladder_term + hole_term).astype(jnp.bfloat16)]
  transfers between devices with their start and end apart: 3 -> 0, of which waited for: 2 -> 0; matrix products, arithmetic and copies ran while one was open for 8% -> 0% of each run, Pallas kernels for 0% -> 0%
where the time goes in v1:
time: 65.8 us; the launch traced here: 65.5 us
  Pallas kernels  58.1 us (88%)
  local copies, waits for them, and re-layouts  7.46 us (11%)
    pallas_call x1, Pallas kernels, per_device(): pl.pallas_call(functools.partial(kernel, (tiles, n_blk, share, width)), o...  58.1 us
    unnamed x9, local copies, waits for them, and re-layouts  7.46 us

profile of v1, /device:TPU:1, one launch (start us, length us, event | category | flops | bytes accessed | tf_op | source)
XLA Modules:
  0.0 65.5 jit_solution(4036313137512275374)
XLA Ops:
  0.0 0.0 copy-start
  0.0 2.3 %copy-done = bf16[3072,48,16]{0,2,1:T(8,128)(2,1)S(1)} copy-done((bf16[3072,48,16]{0,2,1:T(8,128)(2,1)S(1)}, bf16[3072,48,16]{0,2,1:T(8,128)(2,1)}, u32[]{:S(2)}) %copy-start) | copy-done | bytes 4718616
  2.3 0.0 copy-start.1
  2.3 2.3 %copy-done.1 = bf16[48,8,6144]{2,1,0:T(8,128)(2,1)S(1)} copy-done((bf16[48,8,6144]{2,1,0:T(8,128)(2,1)S(1)}, bf16[48,8,6144]{2,1,0:T(8,128)(2,1)}, u32[]{:S(2)}) %copy-start.1) | copy-done | bytes 4718616
  4.7 0.0 copy-start.2
  4.7 1.4 %copy-done.2 = bf16[128,6144]{1,0:T(8,128)(2,1)S(1)} copy-done((bf16[128,6144]{1,0:T(8,128)(2,1)S(1)}, bf16[128,6144]{1,0:T(8,128)(2,1)}, u32[]{:S(2)}) %copy-start.2) | copy-done | bytes 1572888
  6.1 0.0 copy-start.3
  6.1 0.7 %copy-done.3 = s32[48,48]{1,0:T(8,128)S(1)} copy-done((s32[48,48]{1,0:T(8,128)S(1)}, s32[48,48]{1,0:T(8,128)}, u32[]{:S(2)}) %copy-start.3) | copy-done | bytes 9240
  6.8 58.1 %shard_map.46 = bf16[384,128]{1,0:T(8,128)(2,1)S(1)} custom-call(bf16[128,6144]{1,0:T(8,128)(2,1)S(1)} %copy-done.2, s32[48,48]{1,0:T(8,128)S(1)} %copy-done.3, bf16[768,3072]{1,0:T(8,128)(2,1)S(1)} %bitcast.5, bf16[384,6144]{1,0:T(8,128)(2,1)S(1)} %bitcast.6), custom_call_target="tpu_custom_call" | custom-call | flops 1300000000 | bytes 12000000 | tf_op jit(solution)/shard_map/pallas_call | solution.py:264
  64.9 0.6 copy.6
Async XLA Ops:
  0.0 2.3 %copy-start = (bf16[3072,48,16]{0,2,1:T(8,128)(2,1)S(1)}, bf16[3072,48,16]{0,2,1:T(8,128)(2,1)}, u32[]{:S(2)}) copy-start(bf16[3072,48,16]{0,2,1:T(8,128)(2,1)} %param.6) | copy-start | bytes 14155780
  2.3 2.3 %copy-start.1 = (bf16[48,8,6144]{2,1,0:T(8,128)(2,1)S(1)}, bf16[48,8,6144]{2,1,0:T(8,128)(2,1)}, u32[]{:S(2)}) copy-start(bf16[48,8,6144]{2,1,0:T(8,128)(2,1)} %param.7) | copy-start | bytes 14155780
  4.7 1.4 %copy-start.2 = (bf16[128,6144]{1,0:T(8,128)(2,1)S(1)}, bf16[128,6144]{1,0:T(8,128)(2,1)}, u32[]{:S(2)}) copy-start(bf16[128,6144]{1,0:T(8,128)(2,1)} %a_hbm.1) | copy-start | bytes 4718596
  6.1 0.7 %copy-start.3 = (s32[48,48]{1,0:T(8,128)S(1)}, s32[48,48]{1,0:T(8,128)}, u32[]{:S(2)}) copy-start(s32[48,48]{1,0:T(8,128)} %tm_hbm.1) | copy-start | bytes 27652

commit v2 on v1

v2 whole, which is shorter than its diff:
```python
import functools

import jax
import jax.numpy as jnp
from jax import lax
from jax.experimental import pallas as pl
from jax.experimental.pallas import tpu as pltpu
from jax.sharding import PartitionSpec as P

MESH = pl.DeviceIdType.MESH
F32 = jnp.float32
BF16 = jnp.bfloat16


def tile_order_and_mask(tm_ref, pair_index, tiles):
    tm = tm_ref[...]
    lane = lax.broadcasted_iota(jnp.int32, (tiles, tiles), 1)
    sub = lax.broadcasted_iota(jnp.int32, (tiles, tiles), 0)
    score_row = jnp.sum(tm, axis=0, keepdims=True) * tiles + lane[:1]
    spread = jnp.broadcast_to(score_row, (tiles, tiles))
    score_col = jnp.sum(jnp.where(lane == sub, spread, 0), axis=1, keepdims=True)
    rank_col = jnp.sum((spread > score_col).astype(jnp.int32), axis=1, keepdims=True)
    order_row = jnp.sum(jnp.where(rank_col == lane, sub, 0), axis=0, keepdims=True)
    mask_row = tm_ref[pl.ds(pair_index, 1), :]
    mask_col = jnp.sum(
        jnp.where(lane == sub, jnp.broadcast_to(mask_row, (tiles, tiles)), 0), axis=1, keepdims=True)
    kept_row = jnp.sum(jnp.where(rank_col == lane, mask_col, 0), axis=0, keepdims=True)
    return order_row, mask_row, kept_row


def swap_lane_blocks(rows, block):
    n = len(rows)
    width = n * block
    lane = lax.broadcasted_iota(jnp.int32, rows[0].shape, 1) // block
    d = n // 2
    while d:
        keep = (lane & d) == 0
        out = list(rows)
        for a in range(n):
            if a & d:
                continue
            b = a + d
            out[a] = jnp.where(keep, rows[a], pltpu.roll(rows[b], d * block, 1))
            out[b] = jnp.where(keep, pltpu.roll(rows[a], width - d * block, 1), rows[b])
        rows = out
        d //= 2
    return rows


def kernel(dims, a_hbm, tm_hbm, l_hbm, h_hbm, out_ref,
           a_ref, tm_ref, l_ref, h_ref, am_ref, lg_ref, meta_ref, meta_smem,
           hsend, panel, psend, prep, ysend, yrecv, qsend, pfin,
           load_sem, meta_sem, h1_send, h1_recv, ring_send, ring_recv,
           p2_send, p2_recv, p3_send, p3_recv, p4_send, p4_recv):
    tiles, n_blk, share, width = dims
    half_tiles = tiles // 2
    p = lax.axis_index("pair")
    y = lax.axis_index("blk")
    x = lax.axis_index("rep")
    core = lax.rem(p, 2)
    zz = p // 2
    other_x = 1 - x
    up = lax.rem(y + 1, n_blk)
    down = lax.rem(y + n_blk - 1, n_blk)

    loads = [
        pltpu.make_async_copy(tm_hbm, tm_ref, load_sem.at[0]),
        pltpu.make_async_copy(l_hbm, l_ref, load_sem.at[1]),
        pltpu.make_async_copy(h_hbm, h_ref, load_sem.at[2]),
    ]
    loads[0].start()

    @pl.loop(0, tiles)
    def _(v):
        start = pl.multiple_of(v * width, width)
        pltpu.make_async_copy(a_hbm.at[:, pl.ds(start, width)], a_ref.at[v], load_sem.at[3]).start()

    loads[1].start()

    barrier = pltpu.get_barrier_semaphore()

    @pl.loop(1, tiles)
    def _(j):
        q = lax.rem(p + j, tiles)
        pl.semaphore_signal(barrier, inc=1, device_id=(q, y, x), device_id_type=MESH)

    @pl.loop(1, n_blk)
    def _(j):
        pl.semaphore_signal(barrier, inc=1, device_id=(p, lax.rem(y + j, n_blk), x), device_id_type=MESH)

    pl.semaphore_signal(barrier, inc=1, device_id=(p, y, other_x), device_id_type=MESH)

    loads[0].wait()
    order_row, mask_row, kept_row = tile_order_and_mask(tm_ref, p, tiles)
    meta_ref[0:1, 0:tiles] = order_row
    meta_ref[1:2, 0:tiles] = mask_row
    meta_ref[2:3, 0:tiles] = kept_row
    to_smem = pltpu.make_async_copy(meta_ref, meta_smem, meta_sem)
    to_smem.start()
    to_smem.wait()
    pltpu.make_async_copy(a_ref, a_ref, load_sem.at[3]).wait()

    parity = lax.rem(core + x, 2)
    rows16 = pl.ds(pl.multiple_of(y * 16, 16), 16)
    for j in range(half_tiles):
        piece = a_ref[meta_smem[0, 2 * j + parity], rows16, :]
        kept = meta_smem[2, 2 * j + parity].astype(F32)
        hsend[j] = (piece.astype(F32) * kept).astype(BF16)

    pl.semaphore_wait(barrier, tiles - 1 + n_blk - 1 + 1)

    chunk = half_tiles // 2

    @pl.when(x == 0)
    def _():
        pltpu.make_async_copy(hsend.at[zz], panel.at[x, y, 0], h1_recv.at[0]).start()

    @pl.when(x != 0)
    def _():
        pltpu.make_async_remote_copy(
            hsend.at[zz], panel.at[x, y, 0], h1_send, h1_recv.at[0],
            device_id=(2 * zz + parity, y, x), device_id_type=MESH).start()

    for c in range(2):
        @pl.loop(max(1, c * chunk), (c + 1) * chunk)
        def _(k):
            dest = lax.rem(zz + jnp.where(lax.rem(k, 2) == 1, (k + 1) // 2, half_tiles - k // 2), half_tiles)
            pltpu.make_async_remote_copy(
                hsend.at[dest], panel.at[x, y, k], h1_send, h1_recv.at[c],
                device_id=(2 * dest + parity, y, x), device_id_type=MESH).start()

    loads[2].start()

    groups = 3
    per_group = tiles // groups
    step_cols = per_group * share

    def entry(n, pos):
        return 4 * groups * (pos // 4) + 4 * n + pos % 4

    for j in range(half_tiles):
        kept = meta_smem[1, x * half_tiles + j].astype(F32)
        am_ref[:, j * width:(j + 1) * width] = (
            a_ref[x * half_tiles + j].astype(F32) * kept).astype(BF16)
    loads[1].wait()
    p2 = []
    for n in range(groups):
        for pos in range(per_group):
            lg_ref[n, pos * share:(pos + 1) * share, :] = l_ref[meta_smem[0, entry(n, pos)]]
        part = lax.dot_general(
            am_ref[...], lg_ref[n], (((1,), (1,)), ((), ())), preferred_element_type=F32)
        part = part.reshape(n_blk, 2, 8, step_cols)
        for s in range(2):
            psend[n, s] = part[:, s]
        p2.append(pltpu.make_async_remote_copy(
            psend.at[n, other_x], prep.at[n], p2_send.at[n], p2_recv.at[n],
            device_id=(p, y, other_x), device_id_type=MESH))
        p2[n].start()

    copies = {}

    def slot(origin_x, origin_y, first, count):
        return panel.at[origin_x, lax.rem(origin_y + 2 * n_blk, n_blk), pl.ds(first, count)]

    def send(key, ref, to_y, to_x):
        which = len(copies)
        copies[key] = pltpu.make_async_remote_copy(
            ref, ref, ring_send.at[which], ring_recv.at[which],
            device_id=(p, to_y, to_x), device_id_type=MESH)
        copies[key].start()

    def spread_chunk0(step):
        for d in range(2):
            if step > 1:
                copies[("near", step - 1, d)].wait_recv()
            origin = y - (step - 1) if d == 0 else y + (step - 1)
            arrived = slot(x, origin, 0, chunk)
            if step < 4:
                send(("near", step, d), arrived, up if d == 0 else down, x)
            elif step == 4:
                send(("near", step, d), slot(x, origin, d * (chunk // 2), chunk // 2), up if d == 0 else down, x)
            else:
                arrived = slot(x, origin, d * (chunk // 2), chunk // 2)
            if step > 1 or d == 0:
                send(("over", step, d), arrived, y, other_x)

    def spread_chunk1(step, part):
        origin_x = x if part == 0 else other_x
        for d in range(2):
            if step > 1:
                copies[("far", step - 1, part, d)].wait_recv()
            if step == 4 and d != part:
                continue
            origin = y - (step - 1) if d == 0 else y + (step - 1)
            send(("far", step, part, d), slot(origin_x, origin, chunk, chunk), up if d == 0 else down, x)

    def particle_rows(n):
        p2[n].wait_recv()
        ysend[n] = psend[n, x] + prep[n]

        @pl.loop(1, n_blk)
        def _(j):
            dest = lax.rem(y + j, n_blk)
            pltpu.make_async_remote_copy(
                ysend.at[n, dest], yrecv.at[n, y], p3_send.at[n], p3_recv.at[n],
                device_id=(p, dest, x), device_id_type=MESH).start()

        pltpu.make_async_copy(ysend.at[n, y], yrecv.at[n, y], p3_recv.at[n]).start()

    def particle_tiles(n):
        pltpu.make_async_copy(yrecv.at[n], yrecv.at[n], p3_recv.at[n]).wait()
        per = width // share
        for g in range(step_cols // width):
            rows = [yrecv[n, b, :, g * width:(g + 1) * width] for b in range(n_blk)]
            for k, row in enumerate(swap_lane_blocks(rows, share)):
                qsend[entry(n, g * per + k)] = row

        @pl.loop(0, per_group)
        def _(j):
            pos = lax.rem(j + p, per_group)
            q = 4 * groups * (pos // 4) + 4 * n + lax.rem(pos, 4)

            @pl.when(q != p)
            def _():
                pltpu.make_async_remote_copy(
                    qsend.at[q], pfin.at[p], p4_send, p4_recv,
                    device_id=(q, y, x), device_id_type=MESH).start()

            @pl.when(q == p)
            def _():
                pltpu.make_async_copy(qsend.at[q], pfin.at[p], p4_recv).start()

    def pieces_in(c):
        mine = panel.at[x, y, pl.ds(c * chunk, chunk)]
        pltpu.make_async_copy(mine, mine, h1_recv.at[c]).wait()

    pieces_in(0)
    spread_chunk0(1)
    particle_rows(0)
    pieces_in(1)
    send(("swap",), slot(x, y, chunk, chunk), y, other_x)
    spread_chunk1(1, 0)
    spread_chunk0(2)
    particle_rows(1)
    copies[("swap",)].wait_recv()
    spread_chunk1(1, 1)
    spread_chunk0(3)
    particle_rows(2)
    particle_tiles(0)
    spread_chunk1(2, 0)
    spread_chunk0(4)
    spread_chunk1(2, 1)
    particle_tiles(1)
    spread_chunk0(5)
    spread_chunk1(3, 0)
    spread_chunk1(3, 1)
    particle_tiles(2)
    spread_chunk1(4, 0)
    spread_chunk1(4, 1)

    rows_out = out_ref.shape[0]

    def product(c, acc):
        for k in range(c * chunk, (c + 1) * chunk):
            offset = (k + 1) // 2 if k % 2 else half_tiles - k // 2
            source = lax.rem(zz + 2 * half_tiles - offset, half_tiles)
            even = panel[core, :, k].reshape(width, width)
            odd = panel[1 - core, :, k].reshape(width, width)
            acc += jnp.dot(
                h_ref[:, pl.ds(pl.multiple_of(source * 2 * width, 2 * width), 2 * width)],
                jnp.concatenate([even, odd], axis=0), preferred_element_type=F32)
        return acc

    loads[2].wait()
    for key, copy in copies.items():
        if key[0] == "over":
            copy.wait_recv()
    acc = product(0, jnp.zeros((rows_out, width), F32))
    copies[("far", 4, 0, 0)].wait_recv()
    copies[("far", 4, 1, 1)].wait_recv()
    acc = product(1, acc)
    pltpu.make_async_copy(pfin, pfin, p4_recv).wait()
    out_ref[...] = (acc + pfin[...].reshape(rows_out, width)).astype(BF16)

    @pl.when(x == 0)
    def _():
        sent = hsend.at[pl.ds(0, half_tiles - 1)]
        pltpu.make_async_copy(sent, sent, h1_send).wait()

    @pl.when(x != 0)
    def _():
        pltpu.make_async_copy(hsend, hsend, h1_send).wait()

    for copy in list(copies.values()) + p2:
        copy.wait_send()
    for n in range(groups):
        sent = ysend.at[n, pl.ds(0, n_blk - 1)]
        pltpu.make_async_copy(sent, sent, p3_send.at[n]).wait()
    sent = qsend.at[pl.ds(0, tiles - 1)]
    pltpu.make_async_copy(sent, sent, p4_send).wait()


def per_device(amplitudes, tile_map, ladder_ints, hole_ints):
    rows, total = amplitudes.shape
    tiles = tile_map.shape[0]
    width = total // tiles
    half_rows, _, share = ladder_ints.shape
    n_blk = width // share
    local_rows = hole_ints.shape[1]
    ladder = jnp.transpose(ladder_ints, (1, 2, 0))
    holes = hole_ints.reshape(tiles * local_rows, hole_ints.shape[2])
    dma = pltpu.SemaphoreType.DMA
    out = pl.pallas_call(
        functools.partial(kernel, (tiles, n_blk, share, width)),
        out_shape=jax.ShapeDtypeStruct((tiles * local_rows, width), BF16),
        in_specs=[pl.BlockSpec(memory_space=pl.ANY)] * 4,
        out_specs=pl.BlockSpec(memory_space=pltpu.VMEM),
        scratch_shapes=[
            pltpu.VMEM((tiles, rows, width), BF16),
            pltpu.VMEM((tiles, tiles), jnp.int32),
            pltpu.VMEM(ladder.shape, BF16),
            pltpu.VMEM(holes.shape, BF16),
            pltpu.VMEM((rows, half_rows), BF16),
            pltpu.VMEM((3, tiles * share // 3, half_rows), BF16),
            pltpu.VMEM((8, 128), jnp.int32),
            pltpu.SMEM((8, 128), jnp.int32),
            pltpu.VMEM((tiles // 2, 16, width), BF16),
            pltpu.VMEM((2, n_blk, tiles // 2, 16, width), BF16),
            pltpu.VMEM((3, 2, n_blk, 8, tiles * share // 3), F32),
            pltpu.VMEM((3, n_blk, 8, tiles * share // 3), F32),
            pltpu.VMEM((3, n_blk, 8, tiles * share // 3), F32),
            pltpu.VMEM((3, n_blk, 8, tiles * share // 3), F32),
            pltpu.VMEM((tiles, 8, width), F32),
            pltpu.VMEM((tiles, 8, width), F32),
            dma((4,)), dma(()), dma(()), dma((2,)), dma((32,)), dma((32,)),
            dma((3,)), dma((3,)), dma((3,)), dma((3,)), dma(()), dma(()),
        ],
        compiler_params=pltpu.CompilerParams(
            collective_id=0, has_side_effects=True, vmem_limit_bytes=60 * 1024 * 1024),
        cost_estimate=pl.CostEstimate(flops=1_300_000_000, bytes_accessed=12_000_000, transcendentals=0),
    )(amplitudes, tile_map, ladder, holes)
    return out.reshape(1, tiles, local_rows, width)


def solution(mesh):
    placed = (P("pair", None), P(), P("rep", None, "blk"), P(None, ("blk", "rep"), None))
    return jax.shard_map(
        per_device,
        mesh=mesh,
        in_specs=placed,
        out_specs=P("pair", None, ("blk", "rep"), None),
        check_vma=False,
    )
```

time: 65.8 us -> 50.9 us (0.77)
  the two profiles are of different devices: /device:TPU:1 before, /device:TPU:24 now
where the time goes in v2:
time: 50.9 us; the launch traced here: 50.8 us
  Pallas kernels  49.2 us (97%)
  local copies, waits for them, and re-layouts  1.54 us (3%)
    pallas_call x1, Pallas kernels, per_device(): pl.pallas_call(functools.partial(kernel, (tiles, n_blk, share, width)), o...  49.2 us
    unnamed x1, local copies, waits for them, and re-layouts  1.54 us

profile of v2, /device:TPU:24, one launch (start us, length us, event | category | flops | bytes accessed | tf_op | source)
XLA Modules:
  0.0 50.8 jit_solution(16522905364184370326)
XLA Ops:
  0.0 49.2 %shard_map.46 = bf16[384,128]{1,0:T(8,128)(2,1)} custom-call(bf16[128,6144]{1,0:T(8,128)(2,1)} %a_hbm.1, s32[48,48]{1,0:T(8,128)} %tm_hbm.1, bf16[48,16,3072]{2,1,0:T(8,128)(2,1)} %bitcast.3, bf16[384,6144]{1,0:T(8,128)(2,1)} %bitcast.4), custom_call_target="tpu_custom_call" | custom-call | flops 1300000000 | bytes 12000000 | tf_op jit(solution)/shard_map/pallas_call | solution.py:313
  49.2 1.5 %copy.6 = bf16[1,48,8,128]{3,2,1,0:T(8,128)(2,1)} copy(bf16[1,48,8,128]{3,2,1,0:T(8,128)(2,1)} %bitcast.5) | data formatting | bytes 196608

commit v3 on v2

v3 whole, which is shorter than its diff:
```python
import functools

import jax
import jax.numpy as jnp
from jax import lax
from jax.experimental import pallas as pl
from jax.experimental.pallas import tpu as pltpu
from jax.sharding import PartitionSpec as P

MESH = pl.DeviceIdType.MESH
F32 = jnp.float32
BF16 = jnp.bfloat16


def tile_order_and_mask(tm_ref, pair_index, tiles):
    tm = tm_ref[...]
    lane = lax.broadcasted_iota(jnp.int32, (tiles, tiles), 1)
    sub = lax.broadcasted_iota(jnp.int32, (tiles, tiles), 0)
    score_row = jnp.sum(tm, axis=0, keepdims=True) * tiles + lane[:1]
    spread = jnp.broadcast_to(score_row, (tiles, tiles))
    score_col = jnp.sum(jnp.where(lane == sub, spread, 0), axis=1, keepdims=True)
    rank_col = jnp.sum((spread > score_col).astype(jnp.int32), axis=1, keepdims=True)
    order_row = jnp.sum(jnp.where(rank_col == lane, sub, 0), axis=0, keepdims=True)
    return order_row, tm_ref[pl.ds(pair_index, 1), :]


def swap_lane_blocks(rows, block):
    n = len(rows)
    width = n * block
    lane = lax.broadcasted_iota(jnp.int32, rows[0].shape, 1) // block
    d = n // 2
    while d:
        keep = (lane & d) == 0
        out = list(rows)
        for a in range(n):
            if a & d:
                continue
            b = a + d
            out[a] = jnp.where(keep, rows[a], pltpu.roll(rows[b], d * block, 1))
            out[b] = jnp.where(keep, pltpu.roll(rows[a], width - d * block, 1), rows[b])
        rows = out
        d //= 2
    return rows


def kernel(dims, a_hbm, tm_hbm, l_hbm, h_hbm, out_ref,
           a_ref, a16_ref, tm_ref, l_ref, h_ref, am_ref, lg_ref, meta_ref, meta_smem,
           hsend, panel, psend, prep, ysend, yrecv, qsend, pfin,
           load_sem, meta_sem, h1_send, h1_recv, ring_send, ring_recv,
           p2_send, p2_recv, p3_send, p3_recv, p4_send, p4_recv):
    tiles, n_blk, share, width = dims
    half_tiles = tiles // 2
    p = lax.axis_index("pair")
    y = lax.axis_index("blk")
    x = lax.axis_index("rep")
    core = lax.rem(p, 2)
    zz = p // 2
    other_x = 1 - x
    sense = 1 - 2 * core
    up = lax.rem(y + sense + n_blk, n_blk)
    down = lax.rem(y - sense + n_blk, n_blk)

    loads = [
        pltpu.make_async_copy(tm_hbm, tm_ref, load_sem.at[0]),
        pltpu.make_async_copy(l_hbm, l_ref, load_sem.at[1]),
        pltpu.make_async_copy(h_hbm, h_ref, load_sem.at[2]),
        pltpu.make_async_copy(a_hbm, a_ref, load_sem.at[3]),
    ]
    loads[0].start()
    loads[3].start()
    loads[1].start()

    def plane(q):
        return jnp.where(lax.rem(q // 2 + zz, 2) == 0, x, other_x)

    barrier = pltpu.get_barrier_semaphore()

    @pl.loop(1, tiles)
    def _(j):
        q = lax.rem(p + j, tiles)
        pl.semaphore_signal(barrier, inc=1, device_id=(q, y, plane(q)), device_id_type=MESH)

    @pl.loop(1, n_blk)
    def _(j):
        pl.semaphore_signal(barrier, inc=1, device_id=(p, lax.rem(y + j, n_blk), x), device_id_type=MESH)

    pl.semaphore_signal(barrier, inc=1, device_id=(p, y, other_x), device_id_type=MESH)

    loads[0].wait()
    order_row, mask_row = tile_order_and_mask(tm_ref, p, tiles)
    meta_ref[0:1, 0:tiles] = order_row
    meta_ref[1:2, 0:tiles] = mask_row
    to_smem = pltpu.make_async_copy(meta_ref, meta_smem, meta_sem)
    to_smem.start()
    to_smem.wait()
    loads[3].wait()

    parity = lax.rem(core + x, 2)
    rows16 = pl.ds(pl.multiple_of(y * 16, 16), 16)
    for v in range(tiles):
        piece = a_ref[rows16, v * width:(v + 1) * width]
        a16_ref[v] = (piece.astype(F32) * meta_smem[1, v].astype(F32)).astype(BF16)
    for j in range(half_tiles):
        hsend[j] = a16_ref[meta_smem[0, 2 * j + lax.rem(parity + zz + j, 2)]]

    groups = 3
    per_group = tiles // groups
    step_cols = per_group * share

    def entry(n, pos):
        return 4 * groups * (pos // 4) + 4 * n + pos % 4

    def products():
        for j in range(half_tiles):
            kept = meta_smem[1, x * half_tiles + j].astype(F32)
            start = pl.multiple_of((x * half_tiles + j) * width, width)
            am_ref[:, j * width:(j + 1) * width] = (
                a_ref[:, pl.ds(start, width)].astype(F32) * kept).astype(BF16)
        loads[1].wait()
        lane = lax.broadcasted_iota(jnp.int32, (n_blk, 8, step_cols), 2) // (2 * share)
        for n in range(groups):
            for pos in range(per_group):
                lg_ref[n, pos * share:(pos + 1) * share, :] = l_ref[meta_smem[0, entry(n, pos)]]
            part = lax.dot_general(
                am_ref[...], lg_ref[n], (((1,), (1,)), ((), ())), preferred_element_type=F32)
            part = part.reshape(n_blk, 2, 8, step_cols)
            own = (lax.rem(lane, 2) == lax.rem(zz, 2)) == (x == 0)
            psend[n, 0] = jnp.where(own, part[:, 0], part[:, 1])
            psend[n, 1] = jnp.where(own, part[:, 1], part[:, 0])

    first_in = p < 2 * tiles // 3
    pl.when(first_in)(products)
    pl.semaphore_wait(barrier, tiles - 1 + n_blk - 1 + 1)

    group = half_tiles // 4

    @pl.when(x == 0)
    def _():
        pltpu.make_async_copy(hsend.at[zz], panel.at[x, y, 0], h1_recv.at[0]).start()

    @pl.when(x != 0)
    def _():
        pltpu.make_async_remote_copy(
            hsend.at[zz], panel.at[x, y, 0], h1_send, h1_recv.at[0],
            device_id=(2 * zz + parity, y, x), device_id_type=MESH).start()

    @pl.loop(1, half_tiles)
    def _(k):
        dest = lax.rem(zz + jnp.where(lax.rem(k, 2) == 1, (k + 1) // 2, half_tiles - k // 2), half_tiles)
        to_x = plane(2 * dest)
        pltpu.make_async_remote_copy(
            hsend.at[dest], panel.at[to_x, y, k], h1_send, h1_recv.at[k // group],
            device_id=(2 * dest + lax.rem(parity + zz + dest, 2), y, to_x), device_id_type=MESH).start()

    loads[2].start()

    pl.when(jnp.logical_not(first_in))(products)
    p2 = []
    for n in range(groups):
        p2.append(pltpu.make_async_remote_copy(
            psend.at[n, 1], prep.at[n], p2_send.at[n], p2_recv.at[n],
            device_id=(p, y, other_x), device_id_type=MESH))
        p2[n].start()

    copies = {}

    def slot(origin_x, origin_y, first, count):
        return panel.at[origin_x, lax.rem(origin_y + 2 * n_blk, n_blk), pl.ds(first, count)]

    def send(key, ref, to_y, to_x):
        which = len(copies)
        copies[key] = pltpu.make_async_remote_copy(
            ref, ref, ring_send.at[which], ring_recv.at[which],
            device_id=(p, to_y, to_x), device_id_type=MESH)
        copies[key].start()

    def spread(stream, step):
        over = stream < 3
        origin_x = other_x if stream == 4 else x
        last = stream % 2
        if step == 1:
            if stream == 4:
                copies[("swap",)].wait_recv()
            else:
                pieces_in(stream)
        if stream == 3 and step == 1:
            send(("swap",), slot(x, y, 3 * group, group), y, other_x)
        for d in range(2):
            if step == 5 and d != last:
                continue
            if step > 1:
                copies[(stream, step - 1, d)].wait_recv()
            origin = y - sense * (step - 1) if d == 0 else y + sense * (step - 1)
            ref = slot(origin_x, origin, min(stream, 3) * group, group)
            if step < 4 or (step == 4 and d == last):
                send((stream, step, d), ref, up if d == 0 else down, x)
            if over and (step > 1 or d == 0):
                send(("over", stream, step, d), ref, y, other_x)

    def particle_rows(n):
        p2[n].wait_recv()
        ysend[n] = psend[n, 0] + prep[n]

        @pl.loop(1, n_blk)
        def _(j):
            dest = lax.rem(y + sense * j + n_blk, n_blk)
            pltpu.make_async_remote_copy(
                ysend.at[n, dest], yrecv.at[n, y], p3_send.at[n], p3_recv.at[n],
                device_id=(p, dest, x), device_id_type=MESH).start()

        pltpu.make_async_copy(ysend.at[n, y], yrecv.at[n, y], p3_recv.at[n]).start()

    def particle_tiles(n):
        pltpu.make_async_copy(yrecv.at[n], yrecv.at[n], p3_recv.at[n]).wait()
        per = width // share
        for g in range(step_cols // width):
            rows = [yrecv[n, b, :, g * width:(g + 1) * width] for b in range(n_blk)]
            for k, row in enumerate(swap_lane_blocks(rows, share)):
                qsend[entry(n, g * per + k)] = row

        @pl.loop(0, per_group)
        def _(j):
            pos = lax.rem(j + p, per_group)
            q = 4 * groups * (pos // 4) + 4 * n + lax.rem(pos, 4)

            @pl.when(q != p)
            def _():
                pltpu.make_async_remote_copy(
                    qsend.at[q], pfin.at[p], p4_send, p4_recv,
                    device_id=(q, y, plane(q)), device_id_type=MESH).start()

            @pl.when(q == p)
            def _():
                pltpu.make_async_copy(qsend.at[q], pfin.at[p], p4_recv).start()

    def pieces_in(g):
        mine = panel.at[x, y, pl.ds(g * group, group)]
        pltpu.make_async_copy(mine, mine, h1_recv.at[g]).wait()

    spread(0, 1)
    spread(1, 1)
    particle_rows(0)
    spread(0, 2)
    spread(2, 1)
    particle_rows(1)
    spread(1, 2)
    particle_rows(2)
    spread(3, 1)
    spread(0, 3)
    spread(2, 2)
    particle_tiles(0)
    spread(1, 3)
    spread(4, 1)
    particle_tiles(1)
    spread(3, 2)
    spread(0, 4)
    spread(2, 3)
    particle_tiles(2)
    spread(1, 4)
    spread(4, 2)
    spread(3, 3)
    spread(0, 5)
    spread(2, 4)
    spread(1, 5)
    spread(4, 3)
    spread(3, 4)
    spread(2, 5)
    spread(4, 4)

    rows_out = out_ref.shape[0]

    def product(first, last, acc):
        for k in range(first, last):
            offset = (k + 1) // 2 if k % 2 else half_tiles - k // 2
            source = lax.rem(zz + 2 * half_tiles - offset, half_tiles)
            even = panel[core, :, k].reshape(width, width)
            odd = panel[1 - core, :, k].reshape(width, width)
            acc += jnp.dot(
                h_ref[:, pl.ds(pl.multiple_of(source * 2 * width, 2 * width), 2 * width)],
                jnp.concatenate([even, odd], axis=0), preferred_element_type=F32)
        return acc

    loads[2].wait()
    for key, copy in copies.items():
        if key[0] == "over":
            copy.wait_recv()
    acc = product(0, 3 * group, jnp.zeros((rows_out, width), F32))
    copies[(3, 4, 1)].wait_recv()
    copies[(4, 4, 0)].wait_recv()
    acc = product(3 * group, half_tiles, acc)
    pltpu.make_async_copy(pfin, pfin, p4_recv).wait()
    out_ref[...] = (acc + pfin[...].reshape(rows_out, width)).astype(BF16)

    @pl.when(x == 0)
    def _():
        sent = hsend.at[pl.ds(0, half_tiles - 1)]
        pltpu.make_async_copy(sent, sent, h1_send).wait()

    @pl.when(x != 0)
    def _():
        pltpu.make_async_copy(hsend, hsend, h1_send).wait()

    for copy in list(copies.values()) + p2:
        copy.wait_send()
    for n in range(groups):
        sent = ysend.at[n, pl.ds(0, n_blk - 1)]
        pltpu.make_async_copy(sent, sent, p3_send.at[n]).wait()
    sent = qsend.at[pl.ds(0, tiles - 1)]
    pltpu.make_async_copy(sent, sent, p4_send).wait()


def per_device(amplitudes, tile_map, ladder_ints, hole_ints):
    rows, total = amplitudes.shape
    tiles = tile_map.shape[0]
    width = total // tiles
    half_rows, _, share = ladder_ints.shape
    n_blk = width // share
    local_rows = hole_ints.shape[1]
    ladder = jnp.transpose(ladder_ints, (1, 2, 0))
    holes = hole_ints.reshape(tiles * local_rows, hole_ints.shape[2])
    dma = pltpu.SemaphoreType.DMA
    out = pl.pallas_call(
        functools.partial(kernel, (tiles, n_blk, share, width)),
        out_shape=jax.ShapeDtypeStruct((tiles * local_rows, width), BF16),
        in_specs=[pl.BlockSpec(memory_space=pl.ANY)] * 4,
        out_specs=pl.BlockSpec(memory_space=pltpu.VMEM),
        scratch_shapes=[
            pltpu.VMEM(amplitudes.shape, BF16),
            pltpu.VMEM((tiles, 16, width), BF16),
            pltpu.VMEM((tiles, tiles), jnp.int32),
            pltpu.VMEM(ladder.shape, BF16),
            pltpu.VMEM(holes.shape, BF16),
            pltpu.VMEM((rows, half_rows), BF16),
            pltpu.VMEM((3, tiles * share // 3, half_rows), BF16),
            pltpu.VMEM((8, 128), jnp.int32),
            pltpu.SMEM((8, 128), jnp.int32),
            pltpu.VMEM((tiles // 2, 16, width), BF16),
            pltpu.VMEM((2, n_blk, tiles // 2, 16, width), BF16),
            pltpu.VMEM((3, 2, n_blk, 8, tiles * share // 3), F32),
            pltpu.VMEM((3, n_blk, 8, tiles * share // 3), F32),
            pltpu.VMEM((3, n_blk, 8, tiles * share // 3), F32),
            pltpu.VMEM((3, n_blk, 8, tiles * share // 3), F32),
            pltpu.VMEM((tiles, 8, width), F32),
            pltpu.VMEM((tiles, 8, width), F32),
            dma((4,)), dma(()), dma(()), dma((4,)), dma((64,)), dma((64,)),
            dma((3,)), dma((3,)), dma((3,)), dma((3,)), dma(()), dma(()),
        ],
        compiler_params=pltpu.CompilerParams(
            collective_id=0, has_side_effects=True, vmem_limit_bytes=60 * 1024 * 1024),
        cost_estimate=pl.CostEstimate(flops=1_300_000_000, bytes_accessed=12_000_000, transcendentals=0),
    )(amplitudes, tile_map, ladder, holes)
    return out.reshape(1, tiles, local_rows, width)


def solution(mesh):
    placed = (P("pair", None), P(), P("rep", None, "blk"), P(None, ("blk", "rep"), None))
    return jax.shard_map(
        per_device,
        mesh=mesh,
        in_specs=placed,
        out_specs=P("pair", None, ("blk", "rep"), None),
        check_vma=False,
    )
```

time: 50.9 us -> 50.2 us (0.986)
  the two profiles are of different devices: /device:TPU:24 before, /device:TPU:8 now
where the time goes in v3:
time: 50.2 us; the launch traced here: 50 us
  Pallas kernels  48.4 us (96%)
  local copies, waits for them, and re-layouts  1.54 us (3%)
    pallas_call x1, Pallas kernels, per_device(): pl.pallas_call(functools.partial(kernel, (tiles, n_blk, share, width)), o...  48.4 us
    unnamed x1, local copies, waits for them, and re-layouts  1.54 us

profile of v3, /device:TPU:8, one launch (start us, length us, event | category | flops | bytes accessed | tf_op | source)
XLA Modules:
  0.0 50.0 jit_solution(6876948385226856789)
XLA Ops:
  0.0 48.4 %shard_map.46 = bf16[384,128]{1,0:T(8,128)(2,1)} custom-call(bf16[128,6144]{1,0:T(8,128)(2,1)} %a_hbm.1, s32[48,48]{1,0:T(8,128)} %tm_hbm.1, bf16[48,16,3072]{2,1,0:T(8,128)(2,1)} %bitcast.3, bf16[384,6144]{1,0:T(8,128)(2,1)} %bitcast.4), custom_call_target="tpu_custom_call" | custom-call | flops 1300000000 | bytes 12000000 | tf_op jit(solution)/shard_map/pallas_call | solution.py:322
  48.5 1.5 %copy.6 = bf16[1,48,8,128]{3,2,1,0:T(8,128)(2,1)} copy(bf16[1,48,8,128]{3,2,1,0:T(8,128)(2,1)} %bitcast.5) | data formatting | bytes 196608

commit v4 on v3

--- a/solution.py
+++ b/solution.py
@@ -132,7 +132,7 @@
     pl.when(first_in)(products)
     pl.semaphore_wait(barrier, tiles - 1 + n_blk - 1 + 1)
 
-    group = half_tiles // 4
+    bounds = (0, 7, 14, 20, half_tiles)
 
     @pl.when(x == 0)
     def _():
@@ -149,7 +149,7 @@
         dest = lax.rem(zz + jnp.where(lax.rem(k, 2) == 1, (k + 1) // 2, half_tiles - k // 2), half_tiles)
         to_x = plane(2 * dest)
         pltpu.make_async_remote_copy(
-            hsend.at[dest], panel.at[to_x, y, k], h1_send, h1_recv.at[k // group],
+            hsend.at[dest], panel.at[to_x, y, k], h1_send, h1_recv.at[sum(jnp.where(k >= b, 1, 0) for b in bounds[1:4])],
             device_id=(2 * dest + lax.rem(parity + zz + dest, 2), y, to_x), device_id_type=MESH).start()
 
     loads[2].start()
@@ -184,14 +184,15 @@
             else:
                 pieces_in(stream)
         if stream == 3 and step == 1:
-            send(("swap",), slot(x, y, 3 * group, group), y, other_x)
+            send(("swap",), slot(x, y, bounds[3], bounds[4] - bounds[3]), y, other_x)
         for d in range(2):
             if step == 5 and d != last:
                 continue
             if step > 1:
                 copies[(stream, step - 1, d)].wait_recv()
             origin = y - sense * (step - 1) if d == 0 else y + sense * (step - 1)
-            ref = slot(origin_x, origin, min(stream, 3) * group, group)
+            g = min(stream, 3)
+            ref = slot(origin_x, origin, bounds[g], bounds[g + 1] - bounds[g])
             if step < 4 or (step == 4 and d == last):
                 send((stream, step, d), ref, up if d == 0 else down, x)
             if over and (step > 1 or d == 0):
@@ -234,7 +235,7 @@
                 pltpu.make_async_copy(qsend.at[q], pfin.at[p], p4_recv).start()
 
     def pieces_in(g):
-        mine = panel.at[x, y, pl.ds(g * group, group)]
+        mine = panel.at[x, y, pl.ds(bounds[g], bounds[g + 1] - bounds[g])]
         pltpu.make_async_copy(mine, mine, h1_recv.at[g]).wait()
 
     spread(0, 1)
@@ -284,10 +285,10 @@
     for key, copy in copies.items():
         if key[0] == "over":
             copy.wait_recv()
-    acc = product(0, 3 * group, jnp.zeros((rows_out, width), F32))
+    acc = product(0, bounds[3], jnp.zeros((rows_out, width), F32))
     copies[(3, 4, 1)].wait_recv()
     copies[(4, 4, 0)].wait_recv()
-    acc = product(3 * group, half_tiles, acc)
+    acc = product(bounds[3], half_tiles, acc)
     pltpu.make_async_copy(pfin, pfin, p4_recv).wait()
     out_ref[...] = (acc + pfin[...].reshape(rows_out, width)).astype(BF16)
 

time: 50.2 us -> 50 us (level)
  no operation moved by 1% of the time
where the time goes in v4:
time: 50 us; the launch traced here: 49.9 us
  Pallas kernels  48.3 us (97%)
  local copies, waits for them, and re-layouts  1.54 us (3%)
    pallas_call x1, Pallas kernels, per_device(): pl.pallas_call(functools.partial(kernel, (tiles, n_blk, share, width)), o...  48.3 us
    unnamed x1, local copies, waits for them, and re-layouts  1.54 us

profile of v4, /device:TPU:8, one launch (start us, length us, event | category | flops | bytes accessed | tf_op | source)
XLA Modules:
  0.0 49.9 jit_solution(4202249567393297362)
XLA Ops:
  0.0 48.3 %shard_map.46 = bf16[384,128]{1,0:T(8,128)(2,1)} custom-call(bf16[128,6144]{1,0:T(8,128)(2,1)} %a_hbm.1, s32[48,48]{1,0:T(8,128)} %tm_hbm.1, bf16[48,16,3072]{2,1,0:T(8,128)(2,1)} %bitcast.3, bf16[384,6144]{1,0:T(8,128)(2,1)} %bitcast.4), custom_call_target="tpu_custom_call" | custom-call | flops 1300000000 | bytes 12000000 | tf_op jit(solution)/shard_map/pallas_call | solution.py:323
  48.3 1.5 %copy.6 = bf16[1,48,8,128]{3,2,1,0:T(8,128)(2,1)} copy(bf16[1,48,8,128]{3,2,1,0:T(8,128)(2,1)} %bitcast.5) | data formatting | bytes 196608
